TPU v7x, 256 devices: a whole 4x4x8 slice. The times are simulated.
256 devices in a mesh: fluid: 64 (over x, z, core), metal: 4 (over y).
Axes of the slice: x: 4, y: 4, z: 8, core: 2. Of those that a mesh axis runs over, the one named last changes fastest.
Arguments:
- fluid_x: bfloat16 [16384, 512], P('fluid', 'metal'), may hold values from -32 to 32
- metal_x: bfloat16 [8192, 512], P('fluid', 'metal'), may hold values from -32 to 32
- w_rf: bfloat16 [512, 512], P(None, 'metal'), may hold values from -0.5 to 0.5
- w_vf: bfloat16 [512, 512], P(None, 'metal'), may hold values from -0.25 to 0.25
- w_rm: bfloat16 [512, 512], P(None, 'metal'), may hold values from -0.5 to 0.5
- w_vm: bfloat16 [512, 512], P(None, 'metal'), may hold values from -0.25 to 0.25
- fluid_grad: bfloat16 [16384, 512], P('fluid', 'metal'), may hold values from -6 to 6
- metal_grad: bfloat16 [8192, 512], P('fluid', 'metal'), may hold values from -6 to 6
- pair_list: int32 [2048, 2], P('fluid'), may hold values from 0 to 63, as said below
- pair_count: int32 [64], P('fluid'), may hold values from 2 to 32, as said below
Outputs:
- fluid_out: bfloat16 [16384, 512], P('fluid', 'metal')
- metal_out: bfloat16 [8192, 512], P('fluid', 'metal')
- fluid_dx: bfloat16 [16384, 512], P('fluid', 'metal')
- metal_dx: bfloat16 [8192, 512], P('fluid', 'metal')
- weight_grads: float32 [4, 512, 512], P(None, None, 'metal')
Inputs may be any that keep to these rules, and one draw needn't show every extreme that they name: `pair_list`: column 0 is a local fluid block below 2, column 1 a metal block below 64. The first pair_count[d] entries of fluid index d are distinct pairs; every fluid block of every index and every metal block stands in some live entry; entries past the count hold valid indices and are ignored. `pair_count`: some fluid index has all 32 slots live.
All inputs are finite; a program needn't handle non-finite values.
Results may differ from a plain program's by a relative error of at most 0.0179.
The roundings to bfloat16 on the way count: a program that leaves them out, or rounds other values in their place, can miss the bound.
Values may be sent and summed in bfloat16 or wider, within the bound.
No kernel may reach another device: no remote copies, remote signals or barrier semaphores. Data moves between devices by JAX's collectives and lax.ppermute only.
A program may use at most 128 MiB of HBM per device.

v0:
```python
import math

import jax
import jax.numpy as jnp
from jax import lax
from jax.sharding import PartitionSpec as P

D = 512
H = 8
BLK = 128


LOWEST = -1e30


def project(inputs, weight):
    return jnp.dot(inputs, weight, preferred_element_type=jnp.float32).astype(jnp.bfloat16)


def back_project(grads, weight):
    return lax.dot_general(
        grads, weight, (((1,), (1,)), ((), ())), preferred_element_type=jnp.float32
    )


def outer_rows(inputs, grads):
    return lax.dot_general(
        inputs, grads, (((0,), (0,)), ((), ())), preferred_element_type=jnp.float32
    )


def body(fluid_x, metal_x, w_rf, w_vf, w_rm, w_vm, fluid_grad, metal_grad, pair_list, pair_count):
    head_size = D // H
    local_heads = w_rf.shape[1] // head_size
    feature_cols = w_rf.shape[1]
    fluid_rows = fluid_x.shape[0]
    blocks = fluid_rows // BLK
    metal_blocks = lax.axis_size("fluid")
    metal_rows = metal_blocks * BLK
    slot_total = pair_list.shape[0]
    batch_size = math.gcd(slot_total, 16)
    inv_root = 1.0 / math.sqrt(head_size)
    live_count = pair_count[0]
    loop_turns = slot_total // batch_size
    fluid_full, metal_full = (
        lax.all_gather(fluid_x, "metal", axis=1, tiled=True),
        lax.all_gather(metal_x, "metal", axis=1, tiled=True),
    )
    fluid_keys = project(fluid_full, w_rf)
    fluid_values = project(fluid_full, w_vf)
    metal_keys = project(metal_full, w_rm)
    metal_values = project(metal_full, w_vm)
    keys_all, values_all = (
        lax.all_gather(metal_keys, "fluid", axis=0, tiled=True),
        lax.all_gather(metal_values, "fluid", axis=0, tiled=True),
    )
    fkey_tiles = fluid_keys.reshape(blocks, BLK, local_heads, head_size)
    fval_tiles = fluid_values.reshape(blocks, BLK, local_heads, head_size)
    mkey_tiles = keys_all.reshape(metal_blocks, BLK, local_heads, head_size)
    mval_tiles = values_all.reshape(metal_blocks, BLK, local_heads, head_size)

    def batch_pairs(number):
        entries = lax.dynamic_slice_in_dim(pair_list, number * batch_size, batch_size, 0)
        slot_index = number * batch_size + jnp.arange(batch_size, dtype=jnp.int32)
        frows = entries[:, 0]
        mrows = entries[:, 1]
        scores = (
            jnp.einsum(
                "pahd,pbhd->phab",
                fkey_tiles[frows],
                mkey_tiles[mrows],
                preferred_element_type=jnp.float32,
            )
            * inv_root
        )
        return (frows, mrows, slot_index < live_count, scores)

    def max_pass(number, state):
        row_max, col_max = state
        frows, mrows, active, scores = batch_pairs(number)
        live = active[:, None, None]
        row_max = row_max.at[frows].max(jnp.where(live, jnp.max(scores, axis=3), LOWEST))
        col_max = col_max.at[mrows].max(jnp.where(live, jnp.max(scores, axis=2), LOWEST))
        return (row_max, col_max)

    row_max, col_local = lax.fori_loop(
        0,
        loop_turns,
        max_pass,
        (
            jnp.full((blocks, local_heads, BLK), LOWEST, jnp.float32),
            jnp.full((metal_blocks, local_heads, BLK), LOWEST, jnp.float32),
        ),
    )
    col_max = lax.pmax(col_local, "fluid")

    def sum_pass(number, state):
        row_sum, fluid_num, col_sum, metal_num = state
        frows, mrows, active, scores = batch_pairs(number)
        live = active[:, None, None, None]
        row_exp = jnp.where(live, jnp.exp(scores - row_max[frows][:, :, :, None]), 0.0)
        col_exp = jnp.where(live, jnp.exp(scores - col_max[mrows][:, :, None, :]), 0.0)
        row_sum = row_sum.at[frows].add(jnp.sum(row_exp, axis=3))
        col_sum = col_sum.at[mrows].add(jnp.sum(col_exp, axis=2))
        fluid_num = fluid_num.at[frows].add(
            jnp.einsum(
                "phab,pbhd->pahd",
                row_exp.astype(jnp.bfloat16),
                mval_tiles[mrows],
                preferred_element_type=jnp.float32,
            )
        )
        metal_num = metal_num.at[mrows].add(
            jnp.einsum(
                "phab,pahd->pbhd",
                col_exp.astype(jnp.bfloat16),
                fval_tiles[frows],
                preferred_element_type=jnp.float32,
            )
        )
        return (row_sum, fluid_num, col_sum, metal_num)

    row_sum, fluid_num, col_sum, metal_num = lax.fori_loop(
        0,
        loop_turns,
        sum_pass,
        (
            jnp.zeros((blocks, local_heads, BLK), jnp.float32),
            jnp.zeros((blocks, BLK, local_heads, head_size), jnp.float32),
            jnp.zeros((metal_blocks, local_heads, BLK), jnp.float32),
            jnp.zeros((metal_blocks, BLK, local_heads, head_size), jnp.float32),
        ),
    )
    fluid_out = (
        (fluid_num / row_sum.transpose(0, 2, 1)[:, :, :, None])
        .reshape(fluid_rows, feature_cols)
        .astype(jnp.bfloat16)
    )
    num_rows = metal_num.reshape(metal_rows, feature_cols)
    total_rows = col_sum.transpose(0, 2, 1).reshape(metal_rows, local_heads)
    own_num, own_sum = (
        lax.psum_scatter(num_rows, "fluid", scatter_dimension=0, tiled=True),
        lax.psum_scatter(total_rows, "fluid", scatter_dimension=0, tiled=True),
    )
    metal_out = (
        (own_num.reshape(BLK, local_heads, head_size) / own_sum[:, :, None])
        .reshape(BLK, feature_cols)
        .astype(jnp.bfloat16)
    )
    scaled_grad = (
        (metal_grad.astype(jnp.float32).reshape(BLK, local_heads, head_size) / own_sum[:, :, None])
        .reshape(BLK, feature_cols)
        .astype(jnp.bfloat16)
    )
    scaled_all, output_all = (
        lax.all_gather(scaled_grad, "fluid", axis=0, tiled=True),
        lax.all_gather(metal_out, "fluid", axis=0, tiled=True),
    )
    delta_f = jnp.sum(
        (fluid_grad.astype(jnp.float32) * fluid_out.astype(jnp.float32)).reshape(
            fluid_rows, local_heads, head_size
        ),
        axis=2,
    )
    delta_m = jnp.sum(
        (scaled_all.astype(jnp.float32) * output_all.astype(jnp.float32)).reshape(
            metal_blocks, BLK, local_heads, head_size
        ),
        axis=3,
    )
    grad_tiles = fluid_grad.reshape(blocks, BLK, local_heads, head_size)
    scaled_tiles = scaled_all.reshape(metal_blocks, BLK, local_heads, head_size)
    dfluid_tiles = delta_f.reshape(blocks, BLK, local_heads)

    def grad_pass(number, state):
        grad_rf, grad_vf, grad_rm, grad_vm = state
        frows, mrows, active, scores = batch_pairs(number)
        live = active[:, None, None, None]
        attn = jnp.where(
            live,
            jnp.exp(scores - row_max[frows][:, :, :, None]) / row_sum[frows][:, :, :, None],
            0.0,
        )
        col_exp = jnp.where(live, jnp.exp(scores - col_max[mrows][:, :, None, :]), 0.0)
        fluid_term = jnp.einsum(
            "pahd,pbhd->phab",
            grad_tiles[frows],
            mval_tiles[mrows],
            preferred_element_type=jnp.float32,
        )
        metal_term = jnp.einsum(
            "pahd,pbhd->phab",
            fval_tiles[frows],
            scaled_tiles[mrows],
            preferred_element_type=jnp.float32,
        )
        dscore = attn * (fluid_term - dfluid_tiles[frows].transpose(0, 2, 1)[:, :, :, None])
        dscore = dscore + col_exp * (metal_term - delta_m[mrows].transpose(0, 2, 1)[:, :, None, :])
        dscore_weight = dscore.astype(jnp.bfloat16)
        grad_rf = grad_rf.at[frows].add(
            jnp.einsum(
                "phab,pbhd->pahd",
                dscore_weight,
                mkey_tiles[mrows],
                preferred_element_type=jnp.float32,
            )
            * inv_root
        )
        grad_vf = grad_vf.at[frows].add(
            jnp.einsum(
                "phab,pbhd->pahd",
                col_exp.astype(jnp.bfloat16),
                scaled_tiles[mrows],
                preferred_element_type=jnp.float32,
            )
        )
        grad_rm = grad_rm.at[mrows].add(
            jnp.einsum(
                "phab,pahd->pbhd",
                dscore_weight,
                fkey_tiles[frows],
                preferred_element_type=jnp.float32,
            )
            * inv_root
        )
        grad_vm = grad_vm.at[mrows].add(
            jnp.einsum(
                "phab,pahd->pbhd",
                attn.astype(jnp.bfloat16),
                grad_tiles[frows],
                preferred_element_type=jnp.float32,
            )
        )
        return (grad_rf, grad_vf, grad_rm, grad_vm)

    grad_rf, grad_vf, grad_rm, grad_vm = lax.fori_loop(
        0,
        loop_turns,
        grad_pass,
        (
            jnp.zeros((blocks, BLK, local_heads, head_size), jnp.float32),
            jnp.zeros((blocks, BLK, local_heads, head_size), jnp.float32),
            jnp.zeros((metal_blocks, BLK, local_heads, head_size), jnp.float32),
            jnp.zeros((metal_blocks, BLK, local_heads, head_size), jnp.float32),
        ),
    )
    rf_rounded = grad_rf.reshape(fluid_rows, feature_cols).astype(jnp.bfloat16)
    vf_rounded = grad_vf.reshape(fluid_rows, feature_cols).astype(jnp.bfloat16)
    fluid_part = back_project(rf_rounded, w_rf) + back_project(vf_rounded, w_vf)
    fluid_part, weight_rf, weight_vf = (
        fluid_part,
        outer_rows(fluid_full, rf_rounded),
        outer_rows(fluid_full, vf_rounded),
    )
    rm_rounded = lax.psum_scatter(
        grad_rm.reshape(metal_rows, feature_cols), "fluid", scatter_dimension=0, tiled=True
    ).astype(jnp.bfloat16)
    vm_rounded = lax.psum_scatter(
        grad_vm.reshape(metal_rows, feature_cols), "fluid", scatter_dimension=0, tiled=True
    ).astype(jnp.bfloat16)
    metal_part = back_project(rm_rounded, w_rm) + back_project(vm_rounded, w_vm)
    weight_rm = outer_rows(metal_full, rm_rounded)
    weight_vm = outer_rows(metal_full, vm_rounded)
    fluid_dx, metal_dx = (
        lax.psum_scatter(fluid_part, "metal", scatter_dimension=1, tiled=True),
        lax.psum_scatter(metal_part, "metal", scatter_dimension=1, tiled=True),
    )
    weight_grads = lax.psum(jnp.stack([weight_rf, weight_vf, weight_rm, weight_vm]), "fluid")
    return (
        fluid_out,
        metal_out,
        fluid_dx.astype(jnp.bfloat16),
        metal_dx.astype(jnp.bfloat16),
        weight_grads,
    )


def solution(mesh):
    placed = (
        P("fluid", "metal"),
        P("fluid", "metal"),
        P(None, "metal"),
        P(None, "metal"),
        P(None, "metal"),
        P(None, "metal"),
        P("fluid", "metal"),
        P("fluid", "metal"),
        P("fluid", None),
        P("fluid"),
    )
    return jax.shard_map(
        body,
        mesh=mesh,
        in_specs=placed,
        out_specs=(
            P("fluid", "metal"),
            P("fluid", "metal"),
            P("fluid", "metal"),
            P("fluid", "metal"),
            P(None, None, "metal"),
        ),
        check_vma=False,
    )
```

profile of v0, /device:TPU:1, one launch (start us, length us, event | category | flops | bytes accessed | tf_op | source)
XLA Modules:
  0.0 1553.4 jit_solution(13822160661187020611)
XLA Ops:
  7.2 10.3 all_gather.19
  21.1 9.6 all_gather.18
  31.0 70.5 %all-gather.5.cloned.1.call-done = bf16[8192,128]{1,0:T(8,128)(2,1)} async-done(((bf16[128,128]{1,0:T(8,128)(2,1)}), bf16[8192,128]{1,0:T(8,128)(2,1)}) %all-gather.5.cloned.1.call-update) | async-done | bytes 2097168 | tf_op jit(solution)/shard_map/all_gather | solution.py:54
  101.5 8.2 reshape.334
  109.8 23.3 %while.53 = (s32[]{:T(128)}, f32[2,2,128]{2,1,0:T(2,128)S(1)}, f32[64,2,128]{2,1,0:T(2,128)S(1)}, s32[32,2]{0,1:T(2,128)S(1)}, s32[]{:T(128)}, /*index=5*/bf16[2...) while((s32[]{:T(128)}, f32[2,2,128]{2,1,0:T(2,128)S(1)}, ...), condition=%wide.region_5.6_spmd, body=%wide.region_0.5_spmd.sunk | while | flops 68692104 | bytes 3351623 | solution.py:86
  110.6 4.8 gather_fusion
  122.2 4.8 gather_fusion
  134.1 45.8 %all-gather.7.cloned.1.call-done = bf16[8192,128]{1,0:T(8,128)(2,1)} async-done(((bf16[128,128]{1,0:T(8,128)(2,1)}), bf16[8192,128]{1,0:T(8,128)(2,1)}) %all-gather.7.cloned.1.call-update) | async-done | bytes 2097168 | tf_op jit(solution)/shard_map/all_gather | solution.py:55
  179.9 8.3 reshape.335
  188.1 161.4 %all-reduce.3.cloned.1.call-done = f32[64,2,128]{2,1,0:T(2,128)} async-done(((f32[64,2,128]{2,1,0:T(2,128)}), f32[64,2,128]{2,1,0:T(2,128)}) %all-reduce.3.cloned.1.call-update) | async-done | bytes 65552 | tf_op jit(solution)/shard_map/pmax | solution.py:95
  352.0 67.6 %while.54 = (s32[]{:T(128)}, f32[2,2,128]{2,1,0:T(2,128)S(1)}, f32[2,128,2,64]{1,3,2,0:T(8,128)S(1)}, f32[64,2,128]{2,1,0:T(2,128)S(1)}, f32[64,128,2,64]{1,3,2,...) while((s32[]{:T(128)}, f32[2,2,128]{2,1,0:T(2,128)S(1)}, ...), condition=%wide.region_14.15_spmd, body=%wide.region_7.14_spmd.sunk | while | flops 209717376 | bytes 25437748 | solution.py:123
  355.0 4.8 gather_fusion.6
  359.8 5.7 gather_fusion.4
  368.2 3.6 gather_fusion.5
  382.2 3.4 scatter_fusion.5
  388.4 4.8 gather_fusion.6
  393.3 5.7 gather_fusion.4
  401.7 3.6 gather_fusion.5
  422.3 4.6 copy.105
  426.9 5.2 copy.186
  433.0 125.0 %reduce-scatter.19.cloned.1.call-done = f32[128,2]{1,0:T(8,128)} async-done(((f32[8192,2]{1,0:T(8,128)}), f32[128,2]{1,0:T(8,128)}) %reduce-scatter.19.cloned.1.call-update) | async-done | bytes 1040
  558.9 145.1 %reduce-scatter.9.cloned.1.call-done = f32[128,128]{0,1:T(8,128)} async-done(((f32[8192,128]{0,1:T(8,128)}), f32[128,128]{0,1:T(8,128)}) %reduce-scatter.9.cloned.1.call-update) | async-done | bytes 65552 | tf_op jit(solution)/shard_map/reduce_scatter | solution.py:142
  706.8 77.0 %all-gather.9.cloned.1.call-done = bf16[8192,128]{0,1:T(8,128)(2,1)} async-done(((bf16[128,128]{0,1:T(8,128)(2,1)}), bf16[8192,128]{0,1:T(8,128)(2,1)}) %all-gather.9.cloned.1.call-update) | async-done | bytes 2097168 | tf_op jit(solution)/shard_map/all_gather | solution.py:156
  783.8 74.9 %all-gather.11.cloned.1.call-done = bf16[8192,128]{0,1:T(8,128)(2,1)} async-done(((bf16[128,128]{0,1:T(8,128)(2,1)}), bf16[8192,128]{0,1:T(8,128)(2,1)}) %all-gather.11.cloned.1.call-update) | async-done | bytes 2097168 | tf_op jit(solution)/shard_map/all_gather | solution.py:157
  868.7 5.2 copy.114
  878.9 131.7 %while.55 = (s32[]{:T(128)}, f32[2,128,2,64]{1,3,2,0:T(8,128)S(1)}, f32[2,128,2,64]{1,3,2,0:T(8,128)S(1)}, f32[64,128,2,64]{1,3,2,0:T(8,128)}, f32[64,128,2,64]{...) while((s32[]{:T(128)}, f32[2,128,2,64]{1,3,2,0:T(8,128)S(1)}, ...), condition=%wide.region_24.25_spmd, body=%wide.region_19.24_spmd.sunk | while | flops 482347136 | bytes 61189336 | solution.py:236
  885.2 4.8 gather_fusion.11
  891.9 4.8 gather_fusion.10
  896.7 5.7 gather_fusion.8
  904.9 3.6 gather_fusion.13
  908.4 3.6 gather_fusion.12
  914.3 3.6 gather_fusion.9
  937.9 3.4 scatter_fusion.8
  951.0 4.8 gather_fusion.11
  957.6 4.8 gather_fusion.10
  962.5 5.7 gather_fusion.8
  970.6 3.6 gather_fusion.13
  974.2 3.6 gather_fusion.12
  980.1 3.6 gather_fusion.9
  1010.6 4.6 copy.119
  1015.2 5.2 copy.184
  1020.5 4.6 copy.118
  1025.1 5.3 copy.185
  1032.9 125.0 %reduce-scatter.15.cloned.1.call-done = f32[128,128]{0,1:T(8,128)} async-done(((f32[8192,128]{0,1:T(8,128)}), f32[128,128]{0,1:T(8,128)}) %reduce-scatter.15.cloned.1.call-update) | async-done | bytes 65552 | tf_op jit(solution)/shard_map/reduce_scatter | solution.py:258
  1158.9 145.3 %reduce-scatter.13.cloned.1.call-done = f32[128,128]{0,1:T(8,128)} async-done(((f32[8192,128]{0,1:T(8,128)}), f32[128,128]{0,1:T(8,128)}) %reduce-scatter.13.cloned.1.call-update) | async-done | bytes 65552 | tf_op jit(solution)/shard_map/reduce_scatter | solution.py:255
  1309.2 23.4 %reduce-scatter.11.cloned.1.call-done = f32[256,128]{1,0:T(8,128)} async-done(((f32[256,512]{1,0:T(8,128)}), f32[256,128]{1,0:T(8,128)}) %reduce-scatter.11.cloned.1.call-update) | async-done | bytes 131088 | tf_op jit(solution)/shard_map/reduce_scatter | solution.py:265
  1334.1 188.1 %all-reduce.5.cloned.1.call-done = f32[4,512,128]{1,2,0:T(8,128)} async-done(((f32[4,512,128]{1,2,0:T(8,128)}), f32[4,512,128]{1,2,0:T(8,128)}) %all-reduce.5.cloned.1.call-update) | async-done | bytes 1048592 | tf_op jit(solution)/shard_map/psum | solution.py:268
  1524.7 20.0 %reduce-scatter.17.cloned.1.call-done = f32[128,128]{1,0:T(8,128)} async-done(((f32[128,512]{1,0:T(8,128)}), f32[128,128]{1,0:T(8,128)}) %reduce-scatter.17.cloned.1.call-update) | async-done | bytes 65552 | tf_op jit(solution)/shard_map/reduce_scatter | solution.py:266
  (245 shorter events, 167.1 us)
Async XLA Ops:
  7.2 23.5 %copy-start = (bf16[512,128]{1,0:T(8,128)(2,1)S(1)}, bf16[512,128]{1,0:T(8,128)(2,1)}, u32[]{:S(2)}) copy-start(bf16[512,128]{1,0:T(8,128)(2,1)} %param.18) | copy-start | bytes 393220
  7.2 94.4 %all-gather.5.cloned.1.call-start = ((), (), s32[]{:S(2)}) async-start(), calls=%async_computation.6 | async-start | bytes 2129920 | tf_op jit(solution)/shard_map/all_gather | solution.py:54
  17.5 13.2 copy-start.8
  19.3 160.6 %all-gather.7.cloned.1.call-start = ((), (), s32[]{:S(2)}) async-start(), calls=%async_computation.7 | async-start | bytes 2129920 | tf_op jit(solution)/shard_map/all_gather | solution.py:55
  21.1 328.4 %all-reduce.3.cloned.1.call-start = ((), (), s32[]{:S(2)}) async-start(), calls=%async_computation.8 | async-start | bytes 131072 | tf_op jit(solution)/shard_map/pmax | solution.py:95
  30.7 103.1 %copy-start.6 = (bf16[256,512]{1,0:T(8,128)(2,1)}, bf16[256,512]{1,0:T(8,128)(2,1)S(1)}, u32[]{:S(2)}) copy-start(bf16[256,512]{1,0:T(8,128)(2,1)S(1)} %all_gather.18) | copy-start | bytes 786436
  31.0 78.8 %copy-start.22 = (s32[32,2]{0,1:T(2,128)S(1)}, s32[32,2]{0,1:T(2,128)}, u32[]{:S(2)}) copy-start(s32[32,2]{0,1:T(2,128)} %param.24) | copy-start | bytes 772
  109.8 24.0 %copy-start.13 = (bf16[512,128]{1,0:T(8,128)(2,1)S(1)}, bf16[512,128]{1,0:T(8,128)(2,1)}, u32[]{:S(2)}) copy-start(bf16[512,128]{1,0:T(8,128)(2,1)} %param.19) | copy-start | bytes 393220
  133.1 0.6 copy-start.10
  133.7 424.3 %reduce-scatter.19.cloned.1.call-start = ((), (), s32[]{:S(2)}) async-start(), calls=%async_computation.17 | async-start | bytes 4259840
  378.4 3.9 copy-start.1
  411.9 3.9 copy-start.1
  422.3 281.8 %reduce-scatter.9.cloned.1.call-start = ((), (), s32[]{:S(2)}) async-start(), calls=%async_computation.9 | async-start | bytes 4259840 | tf_op jit(solution)/shard_map/reduce_scatter | solution.py:142
  432.1 0.8 copy-start.27
  432.1 274.2 %copy-start.20 = (bf16[256,128]{1,0:T(8,128)(2,1)S(1)}, bf16[256,128]{1,0:T(8,128)(2,1)}, u32[]{:S(2)}) copy-start(bf16[256,128]{1,0:T(8,128)(2,1)} %param.22) | copy-start | bytes 196612
  432.2 351.6 %all-gather.9.cloned.1.call-start = ((), (), s32[]{:S(2)}) async-start(), calls=%async_computation.10 | async-start | bytes 2129920 | tf_op jit(solution)/shard_map/all_gather | solution.py:156
  705.6 153.0 %all-gather.11.cloned.1.call-start = ((), (), s32[]{:S(2)}) async-start(), calls=%async_computation.11 | async-start | bytes 2129920 | tf_op jit(solution)/shard_map/all_gather | solution.py:157
  706.3 451.5 %reduce-scatter.15.cloned.1.call-start = ((), (), s32[]{:S(2)}) async-start(), calls=%async_computation.14 | async-start | bytes 4259840 | tf_op jit(solution)/shard_map/reduce_scatter | solution.py:258
  706.7 154.6 %copy-start.11 = (bf16[2,128,2,64]{1,0,3,2:T(2,128)(2,1)}, bf16[2,128,2,64]{1,0,3,2:T(2,128)(2,1)S(1)}, u32[]{:S(2)}) copy-start(bf16[2,128,2,64]{1,0,3,2:T(2,128)(2,1)S(1)} %copy.104) | copy-start | bytes 196612
  921.2 1.0 copy-start.3
  921.2 1.4 copy-start.4
  921.2 1.4 copy-start.17
  921.2 1.4 copy-start.28
  927.6 1.9 copy-start.26
  935.3 2.6 copy-start.2
  935.3 2.6 copy-start.24
  937.9 3.4 copy-start.5
  986.9 1.0 copy-start.3
  986.9 1.4 copy-start.4
  986.9 1.4 copy-start.17
  986.9 1.4 copy-start.28
  993.4 1.9 copy-start.26
  1001.0 2.6 copy-start.2
  1001.0 2.6 copy-start.24
  1003.7 3.4 copy-start.5
  1020.5 283.8 %reduce-scatter.13.cloned.1.call-start = ((), (), s32[]{:S(2)}) async-start(), calls=%async_computation.13 | async-start | bytes 4259840 | tf_op jit(solution)/shard_map/reduce_scatter | solution.py:255
  1030.4 0.9 copy-start.14
  1030.4 2.0 copy-start.7
  1030.4 302.2 %reduce-scatter.11.cloned.1.call-start = ((), (), s32[]{:S(2)}) async-start(), calls=%async_computation.12 | async-start | bytes 655360 | tf_op jit(solution)/shard_map/reduce_scatter | solution.py:265
  1030.5 127.4 %copy-start.9 = (bf16[128,512]{1,0:T(8,128)(2,1)S(1)}, bf16[128,512]{1,0:T(8,128)(2,1)}, u32[]{:S(2)}) copy-start(bf16[128,512]{1,0:T(8,128)(2,1)} %copy-done.8) | copy-start | bytes 393220
  1032.4 489.8 %all-reduce.5.cloned.1.call-start = ((), (), s32[]{:S(2)}) async-start(), calls=%async_computation.16 | async-start | bytes 2097152 | tf_op jit(solution)/shard_map/psum | solution.py:268
  1032.9 273.6 %copy-start.15 = (bf16[512,128]{1,0:T(8,128)(2,1)S(1)}, bf16[512,128]{1,0:T(8,128)(2,1)}, u32[]{:S(2)}) copy-start(bf16[512,128]{1,0:T(8,128)(2,1)} %param.20) | copy-start | bytes 393220
  1158.9 147.8 %copy-start.16 = (bf16[512,128]{1,0:T(8,128)(2,1)S(1)}, bf16[512,128]{1,0:T(8,128)(2,1)}, u32[]{:S(2)}) copy-start(bf16[512,128]{1,0:T(8,128)(2,1)} %param.21) | copy-start | bytes 393220
  1158.9 147.8 %copy-start.21 = (f32[128,128]{0,1:T(8,128)S(1)}, f32[128,128]{0,1:T(8,128)}, u32[]{:S(2)}) copy-start(f32[128,128]{0,1:T(8,128)} %reduce-scatter.15.cloned.1.call-done) | copy-start | bytes 196612
  1304.2 2.3 copy-start.19
  1305.3 2.4 copy-start.12
  1305.3 3.1 copy-start.18
  1306.4 238.3 %reduce-scatter.17.cloned.1.call-start = ((), (), s32[]{:S(2)}) async-start(), calls=%async_computation.15 | async-start | bytes 327680 | tf_op jit(solution)/shard_map/reduce_scatter | solution.py:266
  (4 other events, 2.3 us)
Sparse Core Ops, SparseCore 0:
  19.4 82.0 all-gather.4
  104.9 74.9 all-gather.6
  183.9 165.4 all-reduce.2
  422.4 135.6 reduce-scatter.18
  562.0 142.0 reduce-scatter.8
  707.4 76.3 all-gather.8
  787.2 71.3 all-gather.10
  1020.6 137.2 reduce-scatter.14
  1162.0 142.1 reduce-scatter.12
  1306.8 25.7 reduce-scatter.10
  1337.0 185.1 all-reduce.4
  1524.5 20.1 reduce-scatter.16
where the time goes:
time: 1570 us; the launch traced here: 1550 us
  waiting for transfers between devices  1200 us (76%)
  local copies, waits for them, and re-layouts  209 us (13%)
  other arithmetic  58.9 us (4%)
  matrix products  46.7 us (3%)
  blocking collectives  19.9 us (1%)
    psum x1, waiting for transfers between devices, body(): lax.psum(jnp.stack([weight_rf, weight_vf, weight_rm, weight_vm]), 'fluid')  188 us
    pmax x1, waiting for transfers between devices, body(): col_max = lax.pmax(col_local, 'fluid')  161 us
    reduce_scatter x1, waiting for transfers between devices, body(): lax.psum_scatter(grad_rm.reshape(metal_rows, feature_cols), 'fluid', scat...  145 us
    reduce_scatter x1, waiting for transfers between devices, body(): lax.psum_scatter(num_rows, 'fluid', scatter_dimension=0, tiled=True)  145 us
    unnamed x13, waiting for transfers between devices  126 us
    reduce_scatter x1, waiting for transfers between devices, body(): lax.psum_scatter(grad_vm.reshape(metal_rows, feature_cols), 'fluid', scat...  125 us
    all_gather x1, waiting for transfers between devices, body(): lax.all_gather(scaled_grad, 'fluid', axis=0, tiled=True)  77 us
    all_gather x1, waiting for transfers between devices, body(): lax.all_gather(metal_out, 'fluid', axis=0, tiled=True)  74.9 us
  transfers between devices with their start and end apart: 12, of which 12 were waited for; matrix products, arithmetic and copies ran while one was open for 5% of the time, Pallas kernels for 0%

commit v1 on v0

v1 whole, which is shorter than its diff:
```python
import functools

import jax
import jax.numpy as jnp
from jax import lax
from jax.experimental import pallas as pl
from jax.experimental.pallas import tpu as pltpu
from jax.sharding import Mesh, PartitionSpec as P

BLK = 128
HEADS = 2
DH = 64
NX, NZ, NC, NM = 4, 8, 2, 4
NG = NX * NC
FB = 2
NA = NG * FB
LOWEST = -1e30
ROOT = 0.125
XC = ("x", "c")
FLUID = ("x", "z", "c")
F_ROWS = 3 * FB * BLK + 16
M_ROWS = 3 * BLK
f32, bf16 = jnp.float32, jnp.bfloat16
PARAMS = pltpu.CompilerParams(vmem_limit_bytes=48 * 2**20)
VMEM = pl.BlockSpec(memory_space=pltpu.VMEM)
SMEM = pl.BlockSpec(memory_space=pltpu.SMEM)


def nn(a, b):
    return lax.dot_general(a, b, (((1,), (0,)), ((), ())), preferred_element_type=f32)


def nt(a, b):
    return lax.dot_general(a, b, (((1,), (1,)), ((), ())), preferred_element_type=f32)


def tn(a, b):
    return lax.dot_general(a, b, (((0,), (0,)), ((), ())), preferred_element_type=f32)


def head_mask(h):
    lane = lax.broadcasted_iota(jnp.int32, (BLK, BLK), 1)
    return lane < DH if h == 0 else lane >= DH


def of_head(tile, h):
    return jnp.where(head_mask(h), tile, jnp.zeros_like(tile))


def project_kernel(count, x, w_rf, w_vf, w_rm, w_vm, f_grad, m_grad, pairs, f_pay, m_pay):
    def project(rows, w):
        total = nn(x[0, rows], w[:BLK])
        for i in range(1, NM):
            total += nn(x[i, rows], w[i * BLK : (i + 1) * BLK])
        return total

    fluid, metal = slice(0, FB * BLK), slice(FB * BLK, FB * BLK + BLK)
    f_pay[0 : FB * BLK] = project(fluid, w_rf).astype(bf16)
    values = project(fluid, w_vf)
    for i in range(FB):
        start = (FB + i) * BLK
        f_pay[start : start + BLK] = values[i * BLK : (i + 1) * BLK].T.astype(bf16)
    f_pay[2 * FB * BLK : 3 * FB * BLK] = f_grad[...]
    slots = pairs.shape[0]
    code = pairs[:, 0:1] * (NX * NZ * NC) + pairs[:, 1:2]
    lane = lax.broadcasted_iota(jnp.int32, (slots, BLK), 1)
    slot = lax.broadcasted_iota(jnp.int32, (slots, BLK), 0)
    hit = jnp.where((code == lane) & (slot < count[0]), 1.0, 0.0)
    table = jnp.max(hit, axis=0, keepdims=True)
    f_pay[3 * FB * BLK :] = jnp.broadcast_to(table, (16, BLK)).astype(bf16)
    m_pay[0:BLK] = project(metal, w_rm).astype(bf16)
    m_pay[BLK : 2 * BLK] = project(metal, w_vm).astype(bf16)
    m_pay[2 * BLK :] = m_grad[...]


def f_tile(f_all, a, part):
    start = pl.multiple_of(part * FB * BLK + lax.rem(a, FB) * BLK, BLK)
    return f_all[lax.div(a, FB), pl.ds(start, BLK), :]


def forward_kernel(at, live, f_all, *refs):
    m_in = refs[:NZ]
    r_stat, c_stat, f_num, m_num, todo = refs[NZ : NZ + 5]
    m_key, m_valt, m_gradt = refs[NZ + 5 :]
    z = at[0]
    for s in range(NZ):
        j = lax.rem(z - s + NZ, NZ)
        m_key[j] = m_in[s][0:BLK]
        m_valt[j] = m_in[s][BLK : 2 * BLK].astype(f32).T.astype(bf16)
        m_gradt[j] = m_in[s][2 * BLK : 3 * BLK].astype(f32).T

    def list_step(i, n):
        todo[n] = i
        return n + live[i]

    total = lax.fori_loop(0, NA * NZ, list_step, 0)
    todo[NA * NZ] = total
    nr, nc = HEADS * NA, HEADS * NZ
    r_stat[0:nr] = jnp.full((nr, BLK), LOWEST, f32)
    r_stat[nr:] = jnp.zeros((2 * nr, BLK), f32)
    c_stat[0:nc] = jnp.full((nc, BLK), LOWEST, f32)
    c_stat[nc:] = jnp.zeros((2 * nc, BLK), f32)
    f_num[...] = jnp.zeros_like(f_num)
    m_num[...] = jnp.zeros_like(m_num)

    def visit(i, _):
        cell = todo[i]
        a, j = lax.div(cell, NZ), lax.rem(cell, NZ)
        key = f_tile(f_all, a, 0) * jnp.asarray(ROOT, bf16)
        valt = f_tile(f_all, a, 1)
        other, othert = m_key[j], m_valt[j]

        def side(scores, stat, row, count, num, at_block, h, weights):
            before = stat[pl.ds(row, 1), :]
            now = jnp.maximum(before, jnp.max(scores, axis=0, keepdims=True))
            fade = jnp.exp(before - now)
            part = jnp.exp(scores - now)
            stat[pl.ds(row, 1), :] = now
            sums = pl.ds(row + count, 1)
            stat[sums, :] = stat[sums, :] * fade + jnp.sum(part, axis=0, keepdims=True)
            rows = slice(h * DH, (h + 1) * DH)
            num[at_block, rows] = num[at_block, rows] * fade + nn(weights[rows], part.astype(bf16))

        for h in range(HEADS):
            own = of_head(key, h)
            side(nt(other, own), r_stat, h * NA + a, nr, f_num, a, h, othert)
            side(nt(own, other), c_stat, h * NZ + j, nc, m_num, j, h, valt)
        return 0

    lax.fori_loop(0, total, visit, 0)
    for a in range(NA):
        start = (2 * FB + a % FB) * BLK
        gradt = f_all[a // FB, start : start + BLK, :].astype(f32).T
        for h in range(HEADS):
            rows = slice(h * DH, (h + 1) * DH)
            row = 2 * nr + h * NA + a
            r_stat[row : row + 1] = jnp.sum(gradt[rows] * f_num[a, rows], axis=0, keepdims=True)
    for j in range(NZ):
        for h in range(HEADS):
            rows = slice(h * DH, (h + 1) * DH)
            row = 2 * nc + h * NZ + j
            c_stat[row : row + 1] = jnp.sum(m_gradt[j, rows] * m_num[j, rows], axis=0, keepdims=True)


def merge(parts, own, n):
    top = functools.reduce(jnp.maximum, [p[0:n] for p in parts])
    fades = [jnp.exp(p[0:n] - top) for p in parts]
    total = functools.reduce(jnp.add, [w * p[n : 2 * n] for w, p in zip(fades, parts)])
    delta = functools.reduce(jnp.add, [w * p[2 * n :] for w, p in zip(fades, parts)])
    safe = jnp.where(total > 0, total, 1.0)
    return top, safe, delta / safe, jnp.exp(own[0:n] - top) / safe


def backward_kernel(at, todo, f_all, r_own, r_all, c_own, f_num, m_num, *refs):
    m_in, c_in = refs[:NZ], refs[NZ : 2 * NZ - 1]
    f_out = refs[2 * NZ - 1]
    m_out = refs[2 * NZ : 3 * NZ]
    (m_key, m_keyt, m_val, m_grad, m_gradt, b_max, b_delta, r_max, r_inv, r_delta, d_rf, d_vf, d_rm, d_vm) = refs[3 * NZ :]
    z = at[0]
    nr, nc = HEADS * NA, HEADS * NZ
    top, total, delta, r_own_w = merge([r_all.at[p] for p in range(NG)], r_own, nr)
    r_max[...] = top
    r_inv[...] = 1.0 / total
    r_delta[...] = delta
    top, total, delta, c_own_w = merge([c_own, *c_in], c_own, nc)
    delta = delta / total
    pad = jnp.zeros((BLK - 3 * nc, BLK), f32)
    down = jnp.concatenate([top, total, delta, pad], axis=0).T
    b_total = []
    for j in range(NZ):
        for h in range(HEADS):
            k = h * NZ + j
            b_max[j, h] = jnp.broadcast_to(down[:, k : k + 1], (BLK, BLK))
            k += 2 * nc
            b_delta[j, h] = jnp.broadcast_to(down[:, k : k + 1], (BLK, BLK))
        k = nc + j
        b_total.append(
            jnp.where(
                head_mask(0),
                jnp.broadcast_to(down[:, k : k + 1], (BLK, BLK)),
                jnp.broadcast_to(down[:, k + NZ : k + NZ + 1], (BLK, BLK)),
            )
        )
    for s in range(NZ):
        j = lax.rem(z - s + NZ, NZ)
        m_key[j] = m_in[s][0:BLK]
        m_keyt[j] = (m_in[s][0:BLK].astype(f32) * ROOT).T.astype(bf16)
        m_val[j] = m_in[s][BLK : 2 * BLK]
        m_grad[j] = m_in[s][2 * BLK : 3 * BLK]
    for j in range(NZ):
        scaled = m_grad[j].astype(f32) / b_total[j]
        m_grad[j] = scaled.astype(bf16)
        m_gradt[j] = m_grad[j].astype(f32).T.astype(bf16)
    for ref in (d_rf, d_vf, d_rm, d_vm):
        ref[...] = jnp.zeros_like(ref)

    def visit(i, _):
        cell = todo[i]
        a, j = lax.div(cell, NZ), lax.rem(cell, NZ)
        key = f_tile(f_all, a, 0) * jnp.asarray(ROOT, bf16)
        valt = f_tile(f_all, a, 1)
        grad = f_tile(f_all, a, 2)
        other, other_val, scaled = m_key[j], m_val[j], m_grad[j]
        keys, grads, dscores, attns = [], [], [], []
        for h in range(HEADS):
            rows = slice(h * DH, (h + 1) * DH)
            row = pl.ds(h * NA + a, 1)
            own, own_grad = of_head(key, h), of_head(grad, h)
            scores = nt(other, own)
            attn = jnp.exp(scores - r_max[row, :]) * r_inv[row, :]
            col = jnp.exp(scores - b_max[j, h])
            dscore = attn * (nt(other_val, own_grad) - r_delta[row, :])
            dscore = dscore + col * (nn(of_head(scaled, h), valt) - b_delta[j, h])
            dscore = dscore.astype(bf16)
            d_rf[a, rows] += nn(m_keyt[j, rows], dscore)
            d_vf[a, rows] += nn(m_gradt[j, rows], col.astype(bf16))
            keys.append(own)
            grads.append(own_grad)
            dscores.append(dscore)
            attns.append(attn.astype(bf16))
        d_rm[j] += nn(jnp.concatenate(dscores, axis=1), jnp.concatenate(keys, axis=0))
        d_vm[j] += nn(jnp.concatenate(attns, axis=1), jnp.concatenate(grads, axis=0))
        return 0

    lax.fori_loop(0, todo[NA * NZ], visit, 0)
    for a in range(NA):
        base = (a % FB) * 3 * BLK
        for h in range(HEADS):
            rows = slice(h * DH, (h + 1) * DH)
            w = r_own_w[h * NA + a : h * NA + a + 1]
            f_out[a // FB, base + h * DH : base + (h + 1) * DH] = (f_num[a, rows] * w).astype(bf16)
        f_out[a // FB, base + BLK : base + 2 * BLK] = d_rf[a].astype(bf16)
        f_out[a // FB, base + 2 * BLK : base + 3 * BLK] = d_vf[a].astype(bf16)
    for j in range(NZ):
        for h in range(HEADS):
            rows = slice(h * DH, (h + 1) * DH)
            w = c_own_w[h * NZ + j : h * NZ + j + 1]
            m_num[j, rows] = m_num[j, rows] * w
    for s in range(NZ):
        j = lax.rem(z + s, NZ)
        m_out[s][0:BLK] = m_num[j].astype(bf16)
        m_out[s][BLK : 2 * BLK] = d_rm[j].astype(bf16)
        m_out[s][2 * BLK : 3 * BLK] = d_vm[j].astype(bf16)


def finish_kernel(f_parts, x, w_rf, w_vf, w_rm, w_vm, *refs):
    m_parts = refs[:NZ]
    fluid_out, metal_out, dx, wg = refs[NZ:]
    f_sum = functools.reduce(jnp.add, [f_parts[p].astype(f32) for p in range(NG)])
    m_sum = functools.reduce(jnp.add, [p[...].astype(f32) for p in m_parts])
    rf, vf = [], []
    for i in range(FB):
        base = i * 3 * BLK
        fluid_out[i * BLK : (i + 1) * BLK] = f_sum[base : base + BLK].T.astype(bf16)
        rf.append(f_sum[base + BLK : base + 2 * BLK].T.astype(bf16))
        vf.append(f_sum[base + 2 * BLK : base + 3 * BLK].T.astype(bf16))
    rf, vf = jnp.concatenate(rf, axis=0), jnp.concatenate(vf, axis=0)
    metal_out[...] = m_sum[0:BLK].T.astype(bf16)
    rm, vm = m_sum[BLK : 2 * BLK].astype(bf16), m_sum[2 * BLK :].astype(bf16)
    split = FB * BLK
    for i in range(NM):
        rows = slice(i * BLK, (i + 1) * BLK)
        dx[i, 0:split] = (nt(rf, w_rf[rows]) + nt(vf, w_vf[rows])).astype(dx.dtype)
        dx[i, split:] = (nt(rm, w_rm[rows]) + nt(vm, w_vm[rows])).astype(dx.dtype)
        fluid, metal = x[i, 0:split], x[i, split:]
        wg[0, rows] = tn(fluid, rf)
        wg[1, rows] = tn(fluid, vf)
        wg[2, rows] = tn(metal, rm)
        wg[3, rows] = tn(metal, vm)


def call(kernel, out, args, smem=0, scratch=(), smem_outs=(), aliases=None):
    out_specs = [SMEM if i in smem_outs else VMEM for i in range(len(out))]
    return pl.pallas_call(
        kernel,
        out_shape=[jax.ShapeDtypeStruct(*o) for o in out],
        in_specs=[SMEM] * smem + [VMEM] * (len(args) - smem),
        out_specs=out_specs,
        scratch_shapes=[pltpu.VMEM(*s) for s in scratch],
        input_output_aliases=aliases or {},
        compiler_params=PARAMS,
    )(*args)


def shift(value, axis, n, s):
    return lax.ppermute(value, axis, [(i, (i + s) % n) for i in range(n)])


def sum_over(a, axis, n):
    i = lax.axis_index(axis)
    parts = a.reshape((n, a.shape[0] // n) + a.shape[1:])
    total = lax.dynamic_index_in_dim(parts, i, 0, False)
    for s in range(1, n):
        total = total + shift(lax.dynamic_index_in_dim(parts, (i + s) % n, 0, False), axis, n, s)
    return total


def spread_over(a, axis, n):
    i = lax.axis_index(axis)
    out = jnp.zeros((n,) + a.shape, a.dtype)
    out = lax.dynamic_update_index_in_dim(out, a, i, 0)
    for s in range(1, n):
        out = lax.dynamic_update_index_in_dim(out, shift(a, axis, n, s), (i - s) % n, 0)
    return out.reshape((n * a.shape[0],) + a.shape[1:])


def body(fluid_x, metal_x, w_rf, w_vf, w_rm, w_vm, fluid_grad, metal_grad, pair_list, pair_count):
    weights = (w_rf, w_vf, w_rm, w_vm)
    z = lax.axis_index("z")
    at = z.reshape(1)
    tokens = jnp.concatenate([fluid_x, metal_x], axis=0)
    x = lax.all_gather(tokens, "m", axis=0)
    f_pay, m_pay = call(
        project_kernel,
        [((F_ROWS, BLK), bf16), ((M_ROWS, BLK), bf16)],
        [pair_count, x, *weights, fluid_grad, metal_grad, pair_list],
        smem=1,
    )
    f_all = lax.all_gather(f_pay, XC, axis=0)
    m_all = [m_pay] + [shift(m_pay, "z", NZ, s) for s in range(1, NZ)]
    table = f_all[:, 3 * FB * BLK, :].reshape(NA, NX, NZ, NC)
    table = lax.dynamic_index_in_dim(table, lax.axis_index("x"), 1, False)
    table = lax.dynamic_index_in_dim(table, lax.axis_index("c"), 2, False)
    live = (table.reshape(NA * NZ) > 0).astype(jnp.int32)
    block = (BLK, BLK)
    r_own, c_own, f_num, m_num, todo = call(
        forward_kernel,
        [
            ((3 * HEADS * NA, BLK), f32),
            ((3 * HEADS * NZ, BLK), f32),
            ((NA, *block), f32),
            ((NZ, *block), f32),
            ((NA * NZ + 8,), jnp.int32),
        ],
        [at, live, f_all, *m_all],
        smem=2,
        scratch=[((NZ, *block), bf16), ((NZ, *block), bf16), ((NZ, *block), f32)],
        smem_outs=(4,),
    )
    r_all = lax.all_gather(r_own, XC, axis=0)
    c_all = [shift(c_own, "z", NZ, s) for s in range(1, NZ)]
    tile_b, tile_f = ((NZ, *block), bf16), ((NZ, HEADS, *block), f32)
    f_part, *m_part = call(
        backward_kernel,
        [((NG, 3 * FB * BLK, BLK), bf16)] + [((M_ROWS, BLK), bf16)] * NZ,
        [at, todo, f_all, r_own, r_all, c_own, f_num, m_num, *m_all, *c_all],
        smem=2,
        scratch=[tile_b] * 5
        + [tile_f] * 2
        + [((HEADS * NA, BLK), f32)] * 3
        + [((NA, *block), f32)] * 2
        + [((NZ, *block), f32)] * 2,
    )
    f_part = lax.all_to_all(f_part, XC, 0, 0)
    m_part = [m_part[0]] + [shift(m_part[s], "z", NZ, s) for s in range(1, NZ)]
    fluid_out, metal_out, dx, wg = call(
        finish_kernel,
        [
            ((FB * BLK, BLK), bf16),
            ((BLK, BLK), bf16),
            ((NM, (FB + 1) * BLK, BLK), bf16),
            ((4, NM * BLK, BLK), f32),
        ],
        [f_part, x, *weights, *m_part],
    )
    dx = jnp.sum(lax.all_to_all(dx, "m", 0, 0).astype(f32), axis=0).astype(bf16)
    wg = wg.reshape(4 * NM * BLK, BLK)
    wg = sum_over(sum_over(sum_over(wg, "c", NC), "x", NX), "z", NZ)
    wg = spread_over(spread_over(spread_over(wg, "z", NZ), "x", NX), "c", NC)
    return fluid_out, metal_out, dx[: FB * BLK], dx[FB * BLK :], wg.reshape(4, NM * BLK, BLK)


def solution(mesh):
    grid = Mesh(mesh.devices.reshape(NX, NZ, NC, NM), ("x", "z", "c", "m"))
    tokens, weight = P(FLUID, "m"), P(None, "m")
    return jax.shard_map(
        body,
        mesh=grid,
        in_specs=(tokens, tokens, weight, weight, weight, weight, tokens, tokens, P(FLUID, None), P(FLUID)),
        out_specs=(tokens, tokens, tokens, tokens, P(None, None, "m")),
        check_vma=False,
    )
```

time: 1570 us -> 268 us (0.17)
  waiting for transfers between devices: 1200 us -> 43.5 us
  local copies, waits for them, and re-layouts: 209 us -> 23.3 us
  starting transfers between devices: 0.49 us -> 119 us
  other arithmetic: 58.9 us -> 1.45 us
  matrix products: 46.7 us -> 0 us
  Pallas kernels: 0 us -> 36.5 us
    reduce_scatter x5 -> x0, waiting for transfers between devices: 459 us -> none  [the longest x1 145 us: body(): lax.psum_scatter(grad_rm.reshape(metal_rows, feature_cols), 'fluid', scat...]
    all_gather x4 -> x1, waiting for transfers between devices: 268 us -> 15.7 us  [body(): f_all = lax.all_gather(f_pay, XC, axis=0)]
    psum x1 -> x0, waiting for transfers between devices: 188 us -> none  [body(): lax.psum(jnp.stack([weight_rf, weight_vf, weight_rm, weight_vm]), 'fluid')]
    pmax x1 -> x0, waiting for transfers between devices: 161 us -> none  [body(): col_max = lax.pmax(col_local, 'fluid')]
    gather x46 -> x0, local copies, waits for them, and re-layouts: 132 us -> none  [the longest x8 24.4 us: batch_pairs(): fkey_tiles[frows]]
    unnamed x13 -> x1, waiting for transfers between devices: 126 us -> 0.02 us
    ppermute x0 -> x43, starting transfers between devices: none -> 109 us  [shift(): return lax.ppermute(value, axis, [(i, (i + s) % n) for i in range(n)])]
    dot_general x34 -> x0, matrix products: 46.7 us -> none  [the longest x6 9.31 us: batch_pairs(): jnp.einsum('pahd,pbhd->phab', fkey_tiles[frows], mkey_tiles[mrows], prefe...]
  transfers between devices with their start and end apart: 12 -> 46, of which waited for: 12 -> 16; matrix products, arithmetic and copies ran while one was open for 5% -> 1% of each run, Pallas kernels for 0% -> 0%
where the time goes in v1:
time: 268 us; the launch traced here: 264 us
  starting transfers between devices  119 us (44%)
  waiting for transfers between devices  43.5 us (16%)
  Pallas kernels  36.5 us (14%)
  blocking collectives  25.3 us (9%)
  local copies, waits for them, and re-layouts  23.3 us (9%)
  between operations  15.4 us (6%)
    ppermute x43, starting transfers between devices, shift(): return lax.ppermute(value, axis, [(i, (i + s) % n) for i in range(n)])  109 us
    pallas_call x4, Pallas kernels, call(): pl.pallas_call(kernel, out_shape=[jax.ShapeDtypeStruct(*o) for o in out],...  36.5 us
    unnamed x57, local copies, waits for them, and re-layouts  20.6 us
    ppermute x43, waiting for transfers between devices, shift(): return lax.ppermute(value, axis, [(i, (i + s) % n) for i in range(n)])  20 us
    all_gather x1, waiting for transfers between devices, body(): f_all = lax.all_gather(f_pay, XC, axis=0)  15.7 us
    all_gather x1, blocking collectives, body(): r_all = lax.all_gather(r_own, XC, axis=0)  13.3 us
    all_gather x1, blocking collectives, body(): x = lax.all_gather(tokens, 'm', axis=0)  12 us
    all_to_all x1, waiting for transfers between devices, body(): dx = jnp.sum(lax.all_to_all(dx, 'm', 0, 0).astype(f32), axis=0).astype(bf16)  7.9 us
  transfers between devices with their start and end apart: 46, of which 16 were waited for; matrix products, arithmetic and copies ran while one was open for 1% of the time, Pallas kernels for 0%

profile of v1, /device:TPU:1, one launch (start us, length us, event | category | flops | bytes accessed | tf_op | source)
XLA Modules:
  0.0 264.0 jit_solution(2839707418746719819)
XLA Ops:
  8.1 12.0 %all-gather = bf16[1536,128]{1,0:T(8,128)(2,1)S(1)} all-gather(bf16[384,128]{1,0:T(8,128)(2,1)S(1)} %pad_maximum_fusion), channel_id=2, replica_groups=mesh['x'=4,'z'=8,'c'=2,'m'=4] {'m'}, dimensions={0}, use_global_device_ids=true | all-gather | bytes 491520 | tf_op jit(solution)/shard_map/all_gather | solution.py:312
  26.7 1.1 shard_map.137
  27.8 1.7 collective-permute-start
  29.5 3.0 %collective-permute-start.1 = (bf16[384,128]{1,0:T(8,128)(2,1)S(1)}, bf16[384,128]{1,0:T(8,128)(2,1)S(1)}, u32[]{:S(2)}, u32[]{:S(2)}) collective-permute-start(bf16[384,128]{1,0:T(8,128)(2,1)S(1)} %get-tuple-element.26.refs_0_), channel_id=1, source_target_pairs={{0,16},{8,24},{16,32},{24,40},{32,48},{40,56},{48,0},{56,8},{1,17}... | collective-permute-start | bytes 294920 | tf_op jit(solution)/shard_map/ppermute | solution.py:286
  32.5 3.8 %collective-permute-start.2 = (bf16[384,128]{1,0:T(8,128)(2,1)S(1)}, bf16[384,128]{1,0:T(8,128)(2,1)S(1)}, u32[]{:S(2)}, u32[]{:S(2)}) collective-permute-start(bf16[384,128]{1,0:T(8,128)(2,1)S(1)} %get-tuple-element.26.refs_0_), channel_id=1, source_target_pairs={{0,24},{8,32},{16,40},{24,48},{32,56},{40,0},{48,8},{56,16},{1,25}... | collective-permute-start | bytes 294920 | tf_op jit(solution)/shard_map/ppermute | solution.py:286
  36.7 4.5 %collective-permute-start.4 = (bf16[384,128]{1,0:T(8,128)(2,1)S(1)}, bf16[384,128]{1,0:T(8,128)(2,1)S(1)}, u32[]{:S(2)}, u32[]{:S(2)}) collective-permute-start(bf16[384,128]{1,0:T(8,128)(2,1)S(1)} %get-tuple-element.26.refs_0_), channel_id=1, source_target_pairs={{0,40},{8,48},{16,56},{24,0},{32,8},{40,16},{48,24},{56,32},{1,41}... | collective-permute-start | bytes 294920 | tf_op jit(solution)/shard_map/ppermute | solution.py:286
  41.2 2.4 collective-permute-start.5
  44.3 15.7 %all-gather.5.cloned.1.call-done = bf16[6272,128]{1,0:T(8,128)(2,1)} async-done(((bf16[784,128]{1,0:T(8,128)(2,1)}), bf16[6272,128]{1,0:T(8,128)(2,1)}) %all-gather.5.cloned.1.call-update) | async-done | bytes 1605648 | tf_op jit(solution)/shard_map/all_gather | solution.py:319
  61.5 1.4 copy-done
  63.0 19.0 %shard_map.138 = (f32[96,128]{1,0:T(8,128)S(1)}, f32[48,128]{1,0:T(8,128)S(1)}, f32[16,128,128]{2,1,0:T(8,128)S(1)}, f32[8,128,128]{2,1,0:T(8,128)S(1)}, s32[136]{0:T(256)S(1)}) custom-call(s32[1]{0:T(128)} %bitcast.at, s32[128]{0:T(128)S(1)} %reshape.40.live, bf16[8,784,128]{2,1,0:T(8,128)(2,1)S(1)} %bitcast.87, ...), custom_call_target="tpu_custom_call" | custom-call | tf_op jit(solution)/shard_map/pallas_call | solution.py:274
  82.2 15.0 %collective-permute-start.12 = (f32[48,128]{1,0:T(8,128)S(1)}, f32[48,128]{1,0:T(8,128)S(1)}, u32[]{:S(2)}, u32[]{:S(2)}) collective-permute-start(f32[48,128]{1,0:T(8,128)S(1)} %get-tuple-element.29.c_own), channel_id=1, source_target_pairs={{0,48},{8,56},{16,0},{24,8},{32,16},{40,24},{48,32},{56,40},{1,49}... | collective-permute-start | bytes 73736 | tf_op jit(solution)/shard_map/ppermute | solution.py:286
  97.2 4.7 %collective-permute-start.13 = (f32[48,128]{1,0:T(8,128)S(1)}, f32[48,128]{1,0:T(8,128)S(1)}, u32[]{:S(2)}, u32[]{:S(2)}) collective-permute-start(f32[48,128]{1,0:T(8,128)S(1)} %get-tuple-element.29.c_own), channel_id=1, source_target_pairs={{0,56},{8,0},{16,8},{24,16},{32,24},{40,32},{48,40},{56,48},{1,57}... | collective-permute-start | bytes 73736 | tf_op jit(solution)/shard_map/ppermute | solution.py:286
  101.9 2.6 collective-permute-start.9
  104.5 13.3 %all-gather.2 = f32[768,128]{1,0:T(8,128)S(1)} all-gather(f32[96,128]{1,0:T(8,128)S(1)} %get-tuple-element.28.r_own), channel_id=4, replica_groups=mesh['x'=4,'z'=8,'c'=2,'m'=4] {'x','c'}, dimensions={0}, use_global_device_ids=true | all-gather | bytes 442368 | tf_op jit(solution)/shard_map/all_gather | solution.py:340
  117.8 14.8 %shard_map.139 = (bf16[8,768,128]{2,1,0:T(8,128)(2,1)}, bf16[384,128]{1,0:T(8,128)(2,1)S(1)}, bf16[384,128]{1,0:T(8,128)(2,1)}, bf16[384,128]{1,0:T(8,128)(2,1)}...) custom-call(s32[1]{0:T(128)} %bitcast.at, ...), custom_call_target="tpu_custom_call" | custom-call | tf_op jit(solution)/shard_map/pallas_call | solution.py:274
  133.2 5.3 %all-to-all-start = ((bf16[8,768,128]{2,1,0:T(8,128)(2,1)}), bf16[8,768,128]{2,1,0:T(8,128)(2,1)S(1)}, u32[]{:S(2)}, u32[]{:S(2)}) async-start(bf16[8,768,128]{2,1,0:T(8,128)(2,1)} %get-tuple-element.32), calls=%async_computation | async-start | bytes 3145728 | tf_op jit(solution)/shard_map/all_to_all | solution.py:354
  138.5 5.6 %collective-permute-start.14 = (bf16[384,128]{1,0:T(8,128)(2,1)}, bf16[384,128]{1,0:T(8,128)(2,1)S(1)}, u32[]{:S(2)}, u32[]{:S(2)}) collective-permute-start(bf16[384,128]{1,0:T(8,128)(2,1)} %get-tuple-element.34), channel_id=1, source_target_pairs={{0,8},{8,16},{16,24},{24,32},{32,40},{40,48},{48,56},{56,0},{1,9},... | collective-permute-start | bytes 294920 | tf_op jit(solution)/shard_map/ppermute | solution.py:286
  144.9 3.2 %collective-permute-start.16 = (bf16[384,128]{1,0:T(8,128)(2,1)S(1)}, bf16[384,128]{1,0:T(8,128)(2,1)S(1)}, u32[]{:S(2)}, u32[]{:S(2)}) collective-permute-start(bf16[384,128]{1,0:T(8,128)(2,1)S(1)} %get-tuple-element.36), channel_id=1, source_target_pairs={{0,24},{8,32},{16,40},{24,48},{32,56},{40,0},{48,8},{56,16},{1,25}... | collective-permute-start | bytes 294920 | tf_op jit(solution)/shard_map/ppermute | solution.py:286
  148.1 1.4 collective-permute-start.17
  149.5 2.9 %collective-permute-start.18 = (bf16[384,128]{1,0:T(8,128)(2,1)S(1)}, bf16[384,128]{1,0:T(8,128)(2,1)S(1)}, u32[]{:S(2)}, u32[]{:S(2)}) collective-permute-start(bf16[384,128]{1,0:T(8,128)(2,1)S(1)} %get-tuple-element.38), channel_id=1, source_target_pairs={{0,40},{8,48},{16,56},{24,0},{32,8},{40,16},{48,24},{56,32},{1,41}... | collective-permute-start | bytes 294920 | tf_op jit(solution)/shard_map/ppermute | solution.py:286
  154.2 6.5 %collective-permute-start.20 = (bf16[384,128]{1,0:T(8,128)(2,1)S(1)}, bf16[384,128]{1,0:T(8,128)(2,1)S(1)}, u32[]{:S(2)}, u32[]{:S(2)}) collective-permute-start(bf16[384,128]{1,0:T(8,128)(2,1)S(1)} %get-tuple-element.40), channel_id=1, source_target_pairs={{0,56},{8,0},{16,8},{24,16},{32,24},{40,32},{48,40},{56,48},{1,57}... | collective-permute-start | bytes 294920 | tf_op jit(solution)/shard_map/ppermute | solution.py:286
  160.7 1.1 collective-permute-done.16.refs_3_
  163.8 2.5 collective-permute-done.19.refs_6_
  166.9 1.4 collective-permute-done.20.refs_7_
  176.1 1.6 shard_map.140
  178.4 1.5 collective-permute-done.21
  180.0 1.5 collective-permute-start.22
  181.5 2.4 collective-permute-start.23
  183.9 1.2 collective-permute-start.24
  186.0 4.0 %collective-permute-done.23 = f32[256,128]{1,0:T(8,128)S(1)} collective-permute-done((f32[256,128]{1,0:T(8,128)S(1)}, f32[256,128]{1,0:T(8,128)S(1)}, u32[]{:S(2)}, u32[]{:S(2)}) %collective-permute-start.23) | collective-permute-done | bytes 131104 | tf_op jit(solution)/shard_map/ppermute | solution.py:286
  190.1 9.5 %collective-permute-start.25 = (f32[32,128]{1,0:T(8,128)S(1)}, f32[32,128]{1,0:T(8,128)S(1)}, u32[]{:S(2)}, u32[]{:S(2)}) collective-permute-start(f32[32,128]{1,0:T(8,128)S(1)} %get-tuple-element.50), channel_id=1, source_target_pairs={{0,8},{8,16},{16,24},{24,32},{32,40},{40,48},{48,56},{56,0},{1,9},... | collective-permute-start | bytes 49160 | tf_op jit(solution)/shard_map/ppermute | solution.py:286
  199.6 2.3 collective-permute-start.26
  201.9 2.8 %collective-permute-start.27 = (f32[32,128]{1,0:T(8,128)S(1)}, f32[32,128]{1,0:T(8,128)S(1)}, u32[]{:S(2)}, u32[]{:S(2)}) collective-permute-start(f32[32,128]{1,0:T(8,128)S(1)} %get-tuple-element.55), channel_id=1, source_target_pairs={{0,24},{8,32},{16,40},{24,48},{32,56},{40,0},{48,8},{56,16},{1,25}... | collective-permute-start | bytes 49160 | tf_op jit(solution)/shard_map/ppermute | solution.py:286
  204.6 1.4 collective-permute-start.28
  206.0 3.3 %collective-permute-start.29 = (f32[32,128]{1,0:T(8,128)S(1)}, f32[32,128]{1,0:T(8,128)S(1)}, u32[]{:S(2)}, u32[]{:S(2)}) collective-permute-start(f32[32,128]{1,0:T(8,128)S(1)} %get-tuple-element.53), channel_id=1, source_target_pairs={{0,40},{8,48},{16,56},{24,0},{32,8},{40,16},{48,24},{56,32},{1,41}... | collective-permute-start | bytes 49160 | tf_op jit(solution)/shard_map/ppermute | solution.py:286
  209.4 2.7 %collective-permute-start.30 = (f32[32,128]{1,0:T(8,128)S(1)}, f32[32,128]{1,0:T(8,128)S(1)}, u32[]{:S(2)}, u32[]{:S(2)}) collective-permute-start(f32[32,128]{1,0:T(8,128)S(1)} %get-tuple-element.52), channel_id=1, source_target_pairs={{0,48},{8,56},{16,0},{24,8},{32,16},{40,24},{48,32},{56,40},{1,49}... | collective-permute-start | bytes 49160 | tf_op jit(solution)/shard_map/ppermute | solution.py:286
  212.1 1.4 collective-permute-done.30
  213.5 1.2 collective-permute-done.31
  214.9 1.1 collective-permute-start.33
  216.0 3.9 %collective-permute-start.34 = (f32[32,128]{1,0:T(8,128)S(1)}, f32[32,128]{1,0:T(8,128)S(1)}, u32[]{:S(2)}, u32[]{:S(2)}) collective-permute-start(f32[32,128]{1,0:T(8,128)S(1)} %get-tuple-element.46), channel_id=1, source_target_pairs={{0,24},{8,32},{16,40},{24,48},{32,56},{40,0},{48,8},{56,16},{1,25}... | collective-permute-start | bytes 49160 | tf_op jit(solution)/shard_map/ppermute | solution.py:286
  220.4 4.1 %collective-permute-start.36 = (f32[32,128]{1,0:T(8,128)S(1)}, f32[32,128]{1,0:T(8,128)S(1)}, u32[]{:S(2)}, u32[]{:S(2)}) collective-permute-start(f32[32,128]{1,0:T(8,128)S(1)} %get-tuple-element.46), channel_id=1, source_target_pairs={{0,40},{8,48},{16,56},{24,0},{32,8},{40,16},{48,24},{56,32},{1,41}... | collective-permute-start | bytes 49160 | tf_op jit(solution)/shard_map/ppermute | solution.py:286
  226.5 1.6 collective-permute-done.37
  229.5 2.2 collective-permute-start.40
  232.5 1.1 collective-permute-done.39
  233.6 1.9 collective-permute-done.40
  235.6 7.0 %collective-permute-start.42 = (f32[1024,128]{1,0:T(8,128)S(1)}, f32[1024,128]{1,0:T(8,128)S(1)}, u32[]{:S(2)}, u32[]{:S(2)}) collective-permute-start(f32[1024,128]{1,0:T(8,128)S(1)} %bitcast.95), channel_id=1, source_target_pairs={{0,4},{4,0},{1,5},{5,1},{2,6},{6,2},{3,7},{7,3},{8,12},{12,8},{9,1... | collective-permute-start | bytes 1572872 | tf_op jit(solution)/shard_map/ppermute | solution.py:286
  242.6 4.0 %all-to-all-start.1 = ((bf16[4,384,128]{2,1,0:T(8,128)(2,1)}), bf16[4,384,128]{2,1,0:T(8,128)(2,1)S(1)}, u32[]{:S(2)}, u32[]{:S(2)}) async-start(bf16[4,384,128]{2,1,0:T(8,128)(2,1)} %get-tuple-element.43), calls=%async_computation.1 | async-start | bytes 786432 | tf_op jit(solution)/shard_map/all_to_all | solution.py:366
  246.6 7.9 %all-to-all-done.1 = bf16[4,384,128]{2,1,0:T(8,128)(2,1)S(1)} async-done(((bf16[4,384,128]{2,1,0:T(8,128)(2,1)}), bf16[4,384,128]{2,1,0:T(8,128)(2,1)S(1)}, u32[]{:S(2)}, u32[]{:S(2)}) %all-to-all-start.1) | async-done | bytes 393248 | tf_op jit(solution)/shard_map/all_to_all | solution.py:366
  (138 shorter events, 32.4 us)
Async XLA Ops:
  7.2 52.8 %all-gather.5.cloned.1.call-start = ((), (), s32[]{:S(2)}) async-start(), calls=%async_computation.2 | async-start | bytes 1806336 | tf_op jit(solution)/shard_map/all_gather | solution.py:319
  27.8 13.4 %collective-permute-start = (bf16[384,128]{1,0:T(8,128)(2,1)S(1)}, bf16[384,128]{1,0:T(8,128)(2,1)S(1)}, u32[]{:S(2)}, u32[]{:S(2)}) collective-permute-start(bf16[384,128]{1,0:T(8,128)(2,1)S(1)} %get-tuple-element.26.refs_0_), channel_id=1, source_target_pairs={{0,8},{8,16},{16,24},{24,32},{32,40},{40,48},{48,56},{56,0},{1,9},... | collective-permute-start | bytes 294920 | tf_op jit(solution)/shard_map/ppermute | solution.py:286
  29.5 14.1 %collective-permute-start.1 = (bf16[384,128]{1,0:T(8,128)(2,1)S(1)}, bf16[384,128]{1,0:T(8,128)(2,1)S(1)}, u32[]{:S(2)}, u32[]{:S(2)}) collective-permute-start(bf16[384,128]{1,0:T(8,128)(2,1)S(1)} %get-tuple-element.26.refs_0_), channel_id=1, source_target_pairs={{0,16},{8,24},{16,32},{24,40},{32,48},{40,56},{48,0},{56,8},{1,17}... | collective-permute-start | bytes 294920 | tf_op jit(solution)/shard_map/ppermute | solution.py:286
  32.5 29.0 %collective-permute-start.2 = (bf16[384,128]{1,0:T(8,128)(2,1)S(1)}, bf16[384,128]{1,0:T(8,128)(2,1)S(1)}, u32[]{:S(2)}, u32[]{:S(2)}) collective-permute-start(bf16[384,128]{1,0:T(8,128)(2,1)S(1)} %get-tuple-element.26.refs_0_), channel_id=1, source_target_pairs={{0,24},{8,32},{16,40},{24,48},{32,56},{40,0},{48,8},{56,16},{1,25}... | collective-permute-start | bytes 294920 | tf_op jit(solution)/shard_map/ppermute | solution.py:286
  36.3 25.2 %collective-permute-start.3 = (bf16[384,128]{1,0:T(8,128)(2,1)S(1)}, bf16[384,128]{1,0:T(8,128)(2,1)S(1)}, u32[]{:S(2)}, u32[]{:S(2)}) collective-permute-start(bf16[384,128]{1,0:T(8,128)(2,1)S(1)} %get-tuple-element.26.refs_0_), channel_id=1, source_target_pairs={{0,32},{8,40},{16,48},{24,56},{32,0},{40,8},{48,16},{56,24},{1,33}... | collective-permute-start | bytes 294920 | tf_op jit(solution)/shard_map/ppermute | solution.py:286
  36.7 24.8 %collective-permute-start.4 = (bf16[384,128]{1,0:T(8,128)(2,1)S(1)}, bf16[384,128]{1,0:T(8,128)(2,1)S(1)}, u32[]{:S(2)}, u32[]{:S(2)}) collective-permute-start(bf16[384,128]{1,0:T(8,128)(2,1)S(1)} %get-tuple-element.26.refs_0_), channel_id=1, source_target_pairs={{0,40},{8,48},{16,56},{24,0},{32,8},{40,16},{48,24},{56,32},{1,41}... | collective-permute-start | bytes 294920 | tf_op jit(solution)/shard_map/ppermute | solution.py:286
  41.2 20.3 %collective-permute-start.5 = (bf16[384,128]{1,0:T(8,128)(2,1)S(1)}, bf16[384,128]{1,0:T(8,128)(2,1)S(1)}, u32[]{:S(2)}, u32[]{:S(2)}) collective-permute-start(bf16[384,128]{1,0:T(8,128)(2,1)S(1)} %get-tuple-element.26.refs_0_), channel_id=1, source_target_pairs={{0,48},{8,56},{16,0},{24,8},{32,16},{40,24},{48,32},{56,40},{1,49}... | collective-permute-start | bytes 294920 | tf_op jit(solution)/shard_map/ppermute | solution.py:286
  43.6 17.9 %collective-permute-start.6 = (bf16[384,128]{1,0:T(8,128)(2,1)S(1)}, bf16[384,128]{1,0:T(8,128)(2,1)S(1)}, u32[]{:S(2)}, u32[]{:S(2)}) collective-permute-start(bf16[384,128]{1,0:T(8,128)(2,1)S(1)} %get-tuple-element.26.refs_0_), channel_id=1, source_target_pairs={{0,56},{8,0},{16,8},{24,16},{32,24},{40,32},{48,40},{56,48},{1,57}... | collective-permute-start | bytes 294920 | tf_op jit(solution)/shard_map/ppermute | solution.py:286
  82.0 19.9 %collective-permute-start.10 = (f32[48,128]{1,0:T(8,128)S(1)}, f32[48,128]{1,0:T(8,128)S(1)}, u32[]{:S(2)}, u32[]{:S(2)}) collective-permute-start(f32[48,128]{1,0:T(8,128)S(1)} %get-tuple-element.29.c_own), channel_id=1, source_target_pairs={{0,32},{8,40},{16,48},{24,56},{32,0},{40,8},{48,16},{56,24},{1,33}... | collective-permute-start | bytes 73736 | tf_op jit(solution)/shard_map/ppermute | solution.py:286
  82.1 19.8 %collective-permute-start.11 = (f32[48,128]{1,0:T(8,128)S(1)}, f32[48,128]{1,0:T(8,128)S(1)}, u32[]{:S(2)}, u32[]{:S(2)}) collective-permute-start(f32[48,128]{1,0:T(8,128)S(1)} %get-tuple-element.29.c_own), channel_id=1, source_target_pairs={{0,40},{8,48},{16,56},{24,0},{32,8},{40,16},{48,24},{56,32},{1,41}... | collective-permute-start | bytes 73736 | tf_op jit(solution)/shard_map/ppermute | solution.py:286
  82.2 35.6 %collective-permute-start.12 = (f32[48,128]{1,0:T(8,128)S(1)}, f32[48,128]{1,0:T(8,128)S(1)}, u32[]{:S(2)}, u32[]{:S(2)}) collective-permute-start(f32[48,128]{1,0:T(8,128)S(1)} %get-tuple-element.29.c_own), channel_id=1, source_target_pairs={{0,48},{8,56},{16,0},{24,8},{32,16},{40,24},{48,32},{56,40},{1,49}... | collective-permute-start | bytes 73736 | tf_op jit(solution)/shard_map/ppermute | solution.py:286
  97.2 20.6 %collective-permute-start.13 = (f32[48,128]{1,0:T(8,128)S(1)}, f32[48,128]{1,0:T(8,128)S(1)}, u32[]{:S(2)}, u32[]{:S(2)}) collective-permute-start(f32[48,128]{1,0:T(8,128)S(1)} %get-tuple-element.29.c_own), channel_id=1, source_target_pairs={{0,56},{8,0},{16,8},{24,16},{32,24},{40,32},{48,40},{56,48},{1,57}... | collective-permute-start | bytes 73736 | tf_op jit(solution)/shard_map/ppermute | solution.py:286
  101.9 15.9 %collective-permute-start.7 = (f32[48,128]{1,0:T(8,128)S(1)}, f32[48,128]{1,0:T(8,128)S(1)}, u32[]{:S(2)}, u32[]{:S(2)}) collective-permute-start(f32[48,128]{1,0:T(8,128)S(1)} %get-tuple-element.29.c_own), channel_id=1, source_target_pairs={{0,8},{8,16},{16,24},{24,32},{32,40},{40,48},{48,56},{56,0},{1,9},... | collective-permute-start | bytes 73736 | tf_op jit(solution)/shard_map/ppermute | solution.py:286
  101.9 15.9 %collective-permute-start.8 = (f32[48,128]{1,0:T(8,128)S(1)}, f32[48,128]{1,0:T(8,128)S(1)}, u32[]{:S(2)}, u32[]{:S(2)}) collective-permute-start(f32[48,128]{1,0:T(8,128)S(1)} %get-tuple-element.29.c_own), channel_id=1, source_target_pairs={{0,16},{8,24},{16,32},{24,40},{32,48},{40,56},{48,0},{56,8},{1,17}... | collective-permute-start | bytes 73736 | tf_op jit(solution)/shard_map/ppermute | solution.py:286
  101.9 15.9 %collective-permute-start.9 = (f32[48,128]{1,0:T(8,128)S(1)}, f32[48,128]{1,0:T(8,128)S(1)}, u32[]{:S(2)}, u32[]{:S(2)}) collective-permute-start(f32[48,128]{1,0:T(8,128)S(1)} %get-tuple-element.29.c_own), channel_id=1, source_target_pairs={{0,24},{8,32},{16,40},{24,48},{32,56},{40,0},{48,8},{56,16},{1,25}... | collective-permute-start | bytes 73736 | tf_op jit(solution)/shard_map/ppermute | solution.py:286
  133.2 35.8 %copy-start.6 = (bf16[512,128]{1,0:T(8,128)(2,1)S(1)}, bf16[512,128]{1,0:T(8,128)(2,1)}, u32[]{:S(2)}) copy-start(bf16[512,128]{1,0:T(8,128)(2,1)} %w_rm.3) | copy-start | bytes 393220
  133.2 35.8 %copy-start.8 = (bf16[512,128]{1,0:T(8,128)(2,1)S(1)}, bf16[512,128]{1,0:T(8,128)(2,1)}, u32[]{:S(2)}) copy-start(bf16[512,128]{1,0:T(8,128)(2,1)} %w_vm.3) | copy-start | bytes 393220
  133.2 35.8 %all-to-all-start = ((bf16[8,768,128]{2,1,0:T(8,128)(2,1)}), bf16[8,768,128]{2,1,0:T(8,128)(2,1)S(1)}, u32[]{:S(2)}, u32[]{:S(2)}) async-start(bf16[8,768,128]{2,1,0:T(8,128)(2,1)} %get-tuple-element.32), calls=%async_computation | async-start | bytes 3145728 | tf_op jit(solution)/shard_map/all_to_all | solution.py:354
  138.5 13.9 %collective-permute-start.14 = (bf16[384,128]{1,0:T(8,128)(2,1)}, bf16[384,128]{1,0:T(8,128)(2,1)S(1)}, u32[]{:S(2)}, u32[]{:S(2)}) collective-permute-start(bf16[384,128]{1,0:T(8,128)(2,1)} %get-tuple-element.34), channel_id=1, source_target_pairs={{0,8},{8,16},{16,24},{24,32},{32,40},{40,48},{48,56},{56,0},{1,9},... | collective-permute-start | bytes 294920 | tf_op jit(solution)/shard_map/ppermute | solution.py:286
  144.1 9.4 %collective-permute-start.15 = (bf16[384,128]{1,0:T(8,128)(2,1)}, bf16[384,128]{1,0:T(8,128)(2,1)S(1)}, u32[]{:S(2)}, u32[]{:S(2)}) collective-permute-start(bf16[384,128]{1,0:T(8,128)(2,1)} %get-tuple-element.35), channel_id=1, source_target_pairs={{0,16},{8,24},{16,32},{24,40},{32,48},{40,56},{48,0},{56,8},{1,17}... | collective-permute-start | bytes 294920 | tf_op jit(solution)/shard_map/ppermute | solution.py:286
  144.9 16.9 %collective-permute-start.16 = (bf16[384,128]{1,0:T(8,128)(2,1)S(1)}, bf16[384,128]{1,0:T(8,128)(2,1)S(1)}, u32[]{:S(2)}, u32[]{:S(2)}) collective-permute-start(bf16[384,128]{1,0:T(8,128)(2,1)S(1)} %get-tuple-element.36), channel_id=1, source_target_pairs={{0,24},{8,32},{16,40},{24,48},{32,56},{40,0},{48,8},{56,16},{1,25}... | collective-permute-start | bytes 294920 | tf_op jit(solution)/shard_map/ppermute | solution.py:286
  148.1 14.4 %collective-permute-start.17 = (bf16[384,128]{1,0:T(8,128)(2,1)S(1)}, bf16[384,128]{1,0:T(8,128)(2,1)S(1)}, u32[]{:S(2)}, u32[]{:S(2)}) collective-permute-start(bf16[384,128]{1,0:T(8,128)(2,1)S(1)} %get-tuple-element.37), channel_id=1, source_target_pairs={{0,32},{8,40},{16,48},{24,56},{32,0},{40,8},{48,16},{56,24},{1,33}... | collective-permute-start | bytes 294920 | tf_op jit(solution)/shard_map/ppermute | solution.py:286
  149.5 13.6 %collective-permute-start.18 = (bf16[384,128]{1,0:T(8,128)(2,1)S(1)}, bf16[384,128]{1,0:T(8,128)(2,1)S(1)}, u32[]{:S(2)}, u32[]{:S(2)}) collective-permute-start(bf16[384,128]{1,0:T(8,128)(2,1)S(1)} %get-tuple-element.38), channel_id=1, source_target_pairs={{0,40},{8,48},{16,56},{24,0},{32,8},{40,16},{48,24},{56,32},{1,41}... | collective-permute-start | bytes 294920 | tf_op jit(solution)/shard_map/ppermute | solution.py:286
  153.0 13.2 %collective-permute-start.19 = (bf16[384,128]{1,0:T(8,128)(2,1)S(1)}, bf16[384,128]{1,0:T(8,128)(2,1)S(1)}, u32[]{:S(2)}, u32[]{:S(2)}) collective-permute-start(bf16[384,128]{1,0:T(8,128)(2,1)S(1)} %get-tuple-element.39), channel_id=1, source_target_pairs={{0,48},{8,56},{16,0},{24,8},{32,16},{40,24},{48,32},{56,40},{1,49}... | collective-permute-start | bytes 294920 | tf_op jit(solution)/shard_map/ppermute | solution.py:286
  154.2 14.1 %collective-permute-start.20 = (bf16[384,128]{1,0:T(8,128)(2,1)S(1)}, bf16[384,128]{1,0:T(8,128)(2,1)S(1)}, u32[]{:S(2)}, u32[]{:S(2)}) collective-permute-start(bf16[384,128]{1,0:T(8,128)(2,1)S(1)} %get-tuple-element.40), channel_id=1, source_target_pairs={{0,56},{8,0},{16,8},{24,16},{32,24},{40,32},{48,40},{56,48},{1,57}... | collective-permute-start | bytes 294920 | tf_op jit(solution)/shard_map/ppermute | solution.py:286
  177.8 2.1 collective-permute-start.21
  180.0 6.0 %collective-permute-start.22 = (f32[256,128]{1,0:T(8,128)S(1)}, f32[256,128]{1,0:T(8,128)S(1)}, u32[]{:S(2)}, u32[]{:S(2)}) collective-permute-start(f32[256,128]{1,0:T(8,128)S(1)} %get-tuple-element.47), channel_id=1, source_target_pairs={{0,64},{64,128},{128,192},{192,0},{1,65},{65,129},{129,193},{193,1... | collective-permute-start | bytes 393224 | tf_op jit(solution)/shard_map/ppermute | solution.py:286
  181.5 8.4 %collective-permute-start.23 = (f32[256,128]{1,0:T(8,128)S(1)}, f32[256,128]{1,0:T(8,128)S(1)}, u32[]{:S(2)}, u32[]{:S(2)}) collective-permute-start(f32[256,128]{1,0:T(8,128)S(1)} %get-tuple-element.49), channel_id=1, source_target_pairs={{0,128},{64,192},{128,0},{192,64},{1,129},{65,193},{129,1},{193,65... | collective-permute-start | bytes 393224 | tf_op jit(solution)/shard_map/ppermute | solution.py:286
  183.9 6.1 %collective-permute-start.24 = (f32[256,128]{1,0:T(8,128)S(1)}, f32[256,128]{1,0:T(8,128)S(1)}, u32[]{:S(2)}, u32[]{:S(2)}) collective-permute-start(f32[256,128]{1,0:T(8,128)S(1)} %get-tuple-element.48), channel_id=1, source_target_pairs={{0,192},{64,0},{128,64},{192,128},{1,193},{65,1},{129,65},{193,129... | collective-permute-start | bytes 393224 | tf_op jit(solution)/shard_map/ppermute | solution.py:286
  190.1 19.3 %collective-permute-start.25 = (f32[32,128]{1,0:T(8,128)S(1)}, f32[32,128]{1,0:T(8,128)S(1)}, u32[]{:S(2)}, u32[]{:S(2)}) collective-permute-start(f32[32,128]{1,0:T(8,128)S(1)} %get-tuple-element.50), channel_id=1, source_target_pairs={{0,8},{8,16},{16,24},{24,32},{32,40},{40,48},{48,56},{56,0},{1,9},... | collective-permute-start | bytes 49160 | tf_op jit(solution)/shard_map/ppermute | solution.py:286
  199.6 12.5 %collective-permute-start.26 = (f32[32,128]{1,0:T(8,128)S(1)}, f32[32,128]{1,0:T(8,128)S(1)}, u32[]{:S(2)}, u32[]{:S(2)}) collective-permute-start(f32[32,128]{1,0:T(8,128)S(1)} %get-tuple-element.56), channel_id=1, source_target_pairs={{0,16},{8,24},{16,32},{24,40},{32,48},{40,56},{48,0},{56,8},{1,17}... | collective-permute-start | bytes 49160 | tf_op jit(solution)/shard_map/ppermute | solution.py:286
  201.9 10.2 %collective-permute-start.27 = (f32[32,128]{1,0:T(8,128)S(1)}, f32[32,128]{1,0:T(8,128)S(1)}, u32[]{:S(2)}, u32[]{:S(2)}) collective-permute-start(f32[32,128]{1,0:T(8,128)S(1)} %get-tuple-element.55), channel_id=1, source_target_pairs={{0,24},{8,32},{16,40},{24,48},{32,56},{40,0},{48,8},{56,16},{1,25}... | collective-permute-start | bytes 49160 | tf_op jit(solution)/shard_map/ppermute | solution.py:286
  204.6 7.4 %collective-permute-start.28 = (f32[32,128]{1,0:T(8,128)S(1)}, f32[32,128]{1,0:T(8,128)S(1)}, u32[]{:S(2)}, u32[]{:S(2)}) collective-permute-start(f32[32,128]{1,0:T(8,128)S(1)} %get-tuple-element.54), channel_id=1, source_target_pairs={{0,32},{8,40},{16,48},{24,56},{32,0},{40,8},{48,16},{56,24},{1,33}... | collective-permute-start | bytes 49160 | tf_op jit(solution)/shard_map/ppermute | solution.py:286
  206.0 6.1 %collective-permute-start.29 = (f32[32,128]{1,0:T(8,128)S(1)}, f32[32,128]{1,0:T(8,128)S(1)}, u32[]{:S(2)}, u32[]{:S(2)}) collective-permute-start(f32[32,128]{1,0:T(8,128)S(1)} %get-tuple-element.53), channel_id=1, source_target_pairs={{0,40},{8,48},{16,56},{24,0},{32,8},{40,16},{48,24},{56,32},{1,41}... | collective-permute-start | bytes 49160 | tf_op jit(solution)/shard_map/ppermute | solution.py:286
  209.4 4.1 %collective-permute-start.30 = (f32[32,128]{1,0:T(8,128)S(1)}, f32[32,128]{1,0:T(8,128)S(1)}, u32[]{:S(2)}, u32[]{:S(2)}) collective-permute-start(f32[32,128]{1,0:T(8,128)S(1)} %get-tuple-element.52), channel_id=1, source_target_pairs={{0,48},{8,56},{16,0},{24,8},{32,16},{40,24},{48,32},{56,40},{1,49}... | collective-permute-start | bytes 49160 | tf_op jit(solution)/shard_map/ppermute | solution.py:286
  212.1 2.6 collective-permute-start.31
  214.7 9.8 %collective-permute-start.32 = (f32[32,128]{1,0:T(8,128)S(1)}, f32[32,128]{1,0:T(8,128)S(1)}, u32[]{:S(2)}, u32[]{:S(2)}) collective-permute-start(f32[32,128]{1,0:T(8,128)S(1)} %get-tuple-element.46), channel_id=1, source_target_pairs={{0,8},{8,16},{16,24},{24,32},{32,40},{40,48},{48,56},{56,0},{1,9},... | collective-permute-start | bytes 49160 | tf_op jit(solution)/shard_map/ppermute | solution.py:286
  214.9 9.7 %collective-permute-start.33 = (f32[32,128]{1,0:T(8,128)S(1)}, f32[32,128]{1,0:T(8,128)S(1)}, u32[]{:S(2)}, u32[]{:S(2)}) collective-permute-start(f32[32,128]{1,0:T(8,128)S(1)} %get-tuple-element.46), channel_id=1, source_target_pairs={{0,16},{8,24},{16,32},{24,40},{32,48},{40,56},{48,0},{56,8},{1,17}... | collective-permute-start | bytes 49160 | tf_op jit(solution)/shard_map/ppermute | solution.py:286
  216.0 9.7 %collective-permute-start.34 = (f32[32,128]{1,0:T(8,128)S(1)}, f32[32,128]{1,0:T(8,128)S(1)}, u32[]{:S(2)}, u32[]{:S(2)}) collective-permute-start(f32[32,128]{1,0:T(8,128)S(1)} %get-tuple-element.46), channel_id=1, source_target_pairs={{0,24},{8,32},{16,40},{24,48},{32,56},{40,0},{48,8},{56,16},{1,25}... | collective-permute-start | bytes 49160 | tf_op jit(solution)/shard_map/ppermute | solution.py:286
  219.9 6.6 %collective-permute-start.35 = (f32[32,128]{1,0:T(8,128)S(1)}, f32[32,128]{1,0:T(8,128)S(1)}, u32[]{:S(2)}, u32[]{:S(2)}) collective-permute-start(f32[32,128]{1,0:T(8,128)S(1)} %get-tuple-element.46), channel_id=1, source_target_pairs={{0,32},{8,40},{16,48},{24,56},{32,0},{40,8},{48,16},{56,24},{1,33}... | collective-permute-start | bytes 49160 | tf_op jit(solution)/shard_map/ppermute | solution.py:286
  220.4 6.1 %collective-permute-start.36 = (f32[32,128]{1,0:T(8,128)S(1)}, f32[32,128]{1,0:T(8,128)S(1)}, u32[]{:S(2)}, u32[]{:S(2)}) collective-permute-start(f32[32,128]{1,0:T(8,128)S(1)} %get-tuple-element.46), channel_id=1, source_target_pairs={{0,40},{8,48},{16,56},{24,0},{32,8},{40,16},{48,24},{56,32},{1,41}... | collective-permute-start | bytes 49160 | tf_op jit(solution)/shard_map/ppermute | solution.py:286
  224.5 3.6 %collective-permute-start.37 = (f32[32,128]{1,0:T(8,128)S(1)}, f32[32,128]{1,0:T(8,128)S(1)}, u32[]{:S(2)}, u32[]{:S(2)}) collective-permute-start(f32[32,128]{1,0:T(8,128)S(1)} %get-tuple-element.46), channel_id=1, source_target_pairs={{0,48},{8,56},{16,0},{24,8},{32,16},{40,24},{48,32},{56,40},{1,49}... | collective-permute-start | bytes 49160 | tf_op jit(solution)/shard_map/ppermute | solution.py:286
  224.7 3.9 %collective-permute-start.38 = (f32[32,128]{1,0:T(8,128)S(1)}, f32[32,128]{1,0:T(8,128)S(1)}, u32[]{:S(2)}, u32[]{:S(2)}) collective-permute-start(f32[32,128]{1,0:T(8,128)S(1)} %get-tuple-element.46), channel_id=1, source_target_pairs={{0,56},{8,0},{16,8},{24,16},{32,24},{40,32},{48,40},{56,48},{1,57}... | collective-permute-start | bytes 49160 | tf_op jit(solution)/shard_map/ppermute | solution.py:286
  228.6 5.0 %collective-permute-start.39 = (f32[256,128]{1,0:T(8,128)S(1)}, f32[256,128]{1,0:T(8,128)S(1)}, u32[]{:S(2)}, u32[]{:S(2)}) collective-permute-start(f32[256,128]{1,0:T(8,128)S(1)} %bitcast.100), channel_id=1, source_target_pairs={{0,64},{64,128},{128,192},{192,0},{1,65},{65,129},{129,193},{193,1... | collective-permute-start | bytes 393224 | tf_op jit(solution)/shard_map/ppermute | solution.py:286
  229.5 6.0 %collective-permute-start.40 = (f32[256,128]{1,0:T(8,128)S(1)}, f32[256,128]{1,0:T(8,128)S(1)}, u32[]{:S(2)}, u32[]{:S(2)}) collective-permute-start(f32[256,128]{1,0:T(8,128)S(1)} %bitcast.101), channel_id=1, source_target_pairs={{0,128},{64,192},{128,0},{192,64},{1,129},{65,193},{129,1},{193,65... | collective-permute-start | bytes 393224 | tf_op jit(solution)/shard_map/ppermute | solution.py:286
  231.8 3.8 %collective-permute-start.41 = (f32[256,128]{1,0:T(8,128)S(1)}, f32[256,128]{1,0:T(8,128)S(1)}, u32[]{:S(2)}, u32[]{:S(2)}) collective-permute-start(f32[256,128]{1,0:T(8,128)S(1)} %bitcast.102), channel_id=1, source_target_pairs={{0,192},{64,0},{128,64},{192,128},{1,193},{65,1},{129,65},{193,129... | collective-permute-start | bytes 393224 | tf_op jit(solution)/shard_map/ppermute | solution.py:286
  235.6 20.3 %collective-permute-start.42 = (f32[1024,128]{1,0:T(8,128)S(1)}, f32[1024,128]{1,0:T(8,128)S(1)}, u32[]{:S(2)}, u32[]{:S(2)}) collective-permute-start(f32[1024,128]{1,0:T(8,128)S(1)} %bitcast.95), channel_id=1, source_target_pairs={{0,4},{4,0},{1,5},{5,1},{2,6},{6,2},{3,7},{7,3},{8,12},{12,8},{9,1... | collective-permute-start | bytes 1572872 | tf_op jit(solution)/shard_map/ppermute | solution.py:286
  242.6 11.9 %all-to-all-start.1 = ((bf16[4,384,128]{2,1,0:T(8,128)(2,1)}), bf16[4,384,128]{2,1,0:T(8,128)(2,1)S(1)}, u32[]{:S(2)}, u32[]{:S(2)}) async-start(bf16[4,384,128]{2,1,0:T(8,128)(2,1)} %get-tuple-element.43), calls=%async_computation.1 | async-start | bytes 786432 | tf_op jit(solution)/shard_map/all_to_all | solution.py:366
  (26 other events, 91.4 us)
Sparse Core Ops, SparseCore 0:
  27.9 32.0 all-gather.4
